TPU v7x, 128 devices: a whole 4x4x4 slice. The times are simulated.
128 devices in a mesh: dp: 16 (over z, x), seq: 8 (over y, core).
Axes of the slice: x: 4, y: 4, z: 4, core: 2. Of those that a mesh axis runs over, the one named last changes fastest.
Arguments:
- hidden: bfloat16 [16, 2, 1024, 5120], P('dp', None, 'seq'), may hold values from -6 to 6
- frozen_queries: bfloat16 [16, 2, 1024, 8192], P('dp', None, 'seq'), may hold values from -120 to 120
- frozen_keys: bfloat16 [16, 2, 1024, 1024], P('dp', None, 'seq'), may hold values from -5 to 5
- frozen_value_matrix: bfloat16 [16, 2, 1024, 1024], P('dp', None, 'seq'), may hold values from -6 to 6
- response_index: int32 [16, 2, 1024], P('dp'), may hold values from 0 to 2, never falling along the last dimension, each value on 1 to 512 neighbouring positions
- partner: int32 [16], P('dp'), may hold values from 0 to 15, as said below
- adapter_down_weight: bfloat16 [5120, 64], replicated, may hold values from -0.078125 to 0.078125
- adapter_up_weight: bfloat16 [64, 1024], replicated, may hold values from -0.75 to 0.75
Outputs:
- attention_out: bfloat16 [16, 2, 1024, 8192], P('dp', None, 'seq')
Inputs may be any that keep to these rules, and one draw needn't show every extreme that they name: partner[r] = r XOR m for one m with 1 <= m < 16, the same for every rank.
All inputs are finite; a program needn't handle non-finite values.
Results may differ from a plain program's by a relative error of at most 0.011.
Values may be sent and summed in bfloat16 or wider, within the bound.
No kernel may reach another device: no remote copies, remote signals or barrier semaphores. Data moves between devices by JAX's collectives and lax.ppermute only.
A program may use at most 128 MiB of HBM per device.

v0:
```python
import functools

import jax
import jax.numpy as jnp
from jax import lax
from jax.experimental import pallas as pl
from jax.experimental.pallas import tpu as pltpu
from jax.sharding import PartitionSpec as P

HEAD = 128
GROUP = 8
KV = 8
ROWS = 128
SPAN = GROUP * HEAD
PAIR = 2
ADAPTER_SCALE = 2.0
EXP2_SCALE = 1.4426950408889634 / HEAD**0.5
MASKED = -jnp.inf
VMEM_LIMIT = 60 << 20
SMALL_VMEM_LIMIT = 24 << 20

KEPT = KV // 2
MOVED = KV // 2
LABELS_AT = MOVED * 2 * ROWS
LABEL_ROWS = 16


def fill_bias(bias_ref, own_at, places, label_at, by_key):
    def label_row(at):
        found = jnp.where(at >= 0, label_at(jnp.maximum(at, 0)).astype(jnp.float32), -1.0)
        return jnp.broadcast_to(found, (ROWS, ROWS))

    mine = label_row(own_at)
    query_label = mine.T
    merged = jnp.where(causal(), mine, label_row(own_at - 4))
    for at, tile in enumerate([merged] + [label_row(place) for place in places]):
        bias = jnp.where(tile == query_label, 0.0, MASKED)
        bias_ref[at] = bias.T if by_key else bias


def other_places(own_at):
    low_core = lax.rem(own_at, 2) == 0
    return own_at - 2, jnp.where(low_core, own_at - 1, own_at - 3), jnp.where(low_core, own_at - 3, own_at - 1)


def causal():
    rows = lax.broadcasted_iota(jnp.int32, (ROWS, ROWS), 0)
    return lax.broadcasted_iota(jnp.int32, (ROWS, ROWS), 1) <= rows


def adapter_kernel(
    place_ref, labels_ref, hidden_ref, down_ref, frozen_ref, key_ref, up_ref, first_query_ref, second_query_ref,
    near_ref, moved_ref, moved_query_ref, bias_zero_ref, bias_one_ref, low_ref,
):
    step = pl.program_id(0)
    for at, query_ref in enumerate((first_query_ref, second_query_ref)):
        moved_query_ref[:, at * SPAN : (at + 1) * SPAN] = query_ref[...]

    @pl.when(step == 0)
    def _():
        low_ref[...] = jnp.zeros_like(low_ref)
        own_at = place_ref[0]
        for half, bias_ref in enumerate((bias_zero_ref, bias_one_ref)):
            label_at = lambda at: labels_ref[half : half + 1, pl.ds(pl.multiple_of(at * ROWS, ROWS), ROWS)]
            fill_bias(bias_ref, own_at, other_places(own_at), label_at, half == 1)

    low_ref[...] += lax.dot_general(
        hidden_ref[...].reshape(2 * ROWS, hidden_ref.shape[-1]),
        down_ref[...],
        (((1,), (1,)), ((), ())),
        preferred_element_type=jnp.float32,
    )

    @pl.when(step == pl.num_programs(0) - 1)
    def _():
        low = low_ref[...].astype(jnp.bfloat16)
        delta = jnp.dot(low, up_ref[...], preferred_element_type=jnp.float32)
        for half in range(2):
            own = delta[half * ROWS : (half + 1) * ROWS]
            values = (frozen_ref[half].astype(jnp.float32) + ADAPTER_SCALE * own).astype(jnp.bfloat16)
            for head in range(KV):
                cols = slice(head * HEAD, (head + 1) * HEAD)
                key = key_ref[half, :, cols]
                value = values[:, cols]
                if half == 1 and head % 2 == 1:
                    at = (head - 1) * ROWS
                    moved_ref[at : at + ROWS, :] = key
                    moved_ref[at + ROWS : at + 2 * ROWS, :] = value
                else:
                    at = (head if half == 1 else 2 * (KEPT + head)) * HEAD
                    near_ref[:, at : at + HEAD] = key
                    near_ref[:, at + HEAD : at + 2 * HEAD] = value
        labels = [labels_ref[1:2, at * ROWS : (at + 1) * ROWS].astype(jnp.float32) for at in range(8)]
        labels = jnp.concatenate(labels + [jnp.zeros((LABEL_ROWS - 8, HEAD), jnp.float32)], axis=0)
        moved_ref[LABELS_AT:, :] = labels.astype(jnp.bfloat16)


def adapter(place, labels, hidden, frozen_values, keys, down, up, queries):
    width = hidden.shape[-1]
    steps = MOVED // 2
    part = width // steps
    rank = down.shape[0]
    shapes = [
        ((ROWS, (KEPT + KV) * 2 * HEAD), jnp.bfloat16),
        ((LABELS_AT + LABEL_ROWS, HEAD), jnp.bfloat16),
        ((ROWS, MOVED * SPAN), jnp.bfloat16),
        ((4, ROWS, ROWS), jnp.float32),
        ((4, ROWS, ROWS), jnp.float32),
    ]
    return pl.pallas_call(
        adapter_kernel,
        grid_spec=pltpu.PrefetchScalarGridSpec(
            num_scalar_prefetch=1,
            grid=(steps,),
            in_specs=[
                pl.BlockSpec((None, 2, 8 * ROWS), lambda i, p: (0, 0, 0)),
                pl.BlockSpec((None, 2, ROWS, part), lambda i, p: (0, 0, 0, i)),
                pl.BlockSpec((rank, part), lambda i, p: (0, i)),
                pl.BlockSpec((None, 2, ROWS, KV * HEAD), lambda i, p: (0, 0, 0, 0)),
                pl.BlockSpec((None, 2, ROWS, KV * HEAD), lambda i, p: (0, 0, 0, 0)),
                pl.BlockSpec((rank, KV * HEAD), lambda i, p: (0, 0)),
                pl.BlockSpec((None, None, ROWS, SPAN), lambda i, p: (0, 1, 0, 4 * i + 1)),
                pl.BlockSpec((None, None, ROWS, SPAN), lambda i, p: (0, 1, 0, 4 * i + 3)),
            ],
            out_specs=[
                pl.BlockSpec((ROWS, 2 * SPAN), lambda i, p: (0, i))
                if at == 2
                else pl.BlockSpec(shape, lambda i, p, n=len(shape): (0,) * n)
                for at, (shape, _) in enumerate(shapes)
            ],
            scratch_shapes=[pltpu.VMEM((2 * ROWS, rank), jnp.float32)],
        ),
        out_shape=[jax.ShapeDtypeStruct(*shape) for shape in shapes],
        compiler_params=pltpu.CompilerParams(vmem_limit_bytes=60 << 20),
        cost_estimate=pl.CostEstimate(flops=1 << 20, bytes_accessed=1 << 20, transcendentals=0),
        name="adapter",
    )(place, labels, hidden, down, frozen_values, keys, up, queries, queries)


def near_attention_kernel(by_key, bias_ref, query_ref, own_ref, far_ref, two_ref, pair_ref, out_ref, key_ref, value_ref):
    blocks = [(block, (at, 0), (at, HEAD)) for block, at in ((own_ref, 0), (far_ref, 0), (two_ref, 0), (pair_ref, 0), (pair_ref, ROWS))]
    attend = attend_by_key if by_key else attend_by_query
    attend(bias_ref, query_ref, blocks, out_ref, 0, key_ref, value_ref)


def moved_attention_kernel(
    place_ref, label_ref, query_ref, own_ref, far_ref, two_ref, x_ref, w_ref, came_ref, _,
    out_ref, bias_ref, key_ref, value_ref,
):
    @pl.when(pl.program_id(0) == 0)
    def _():
        own_at = place_ref[0]
        rows = label_ref[...].astype(jnp.float32)
        chosen = lax.broadcasted_iota(jnp.int32, rows.shape, 0)

        def label_at(at):
            return jnp.sum(jnp.where(chosen == at, rows, 0.0), axis=0, keepdims=True)

        fill_bias(bias_ref, own_at, other_places(own_at), label_at, True)

    out_ref[:, :SPAN] = came_ref[...]
    blocks = [(block, (0, 0), (ROWS, 0)) for block in (own_ref, far_ref, two_ref, x_ref, w_ref)]
    attend_by_key(bias_ref, query_ref, blocks, out_ref, GROUP, key_ref, value_ref)


def tile_of(block, corner):
    return block[corner[0] : corner[0] + ROWS, corner[1] : corner[1] + HEAD]


def attend_by_key(bias_ref, query_ref, blocks, out_ref, out_head, key_ref, value_ref):
    is_causal = causal().T

    @pl.when(pl.program_id(0) == 0)
    def _():
        value_ref[HEAD:, :] = jnp.ones((ONES, 5 * ROWS), jnp.bfloat16)

    for at, (block, key_at, value_at) in enumerate(blocks):
        span = slice(at * ROWS, (at + 1) * ROWS)
        key_ref[span, :] = tile_of(block, key_at)
        value_ref[:HEAD, span] = tile_of(block, value_at).T
    queries = jnp.concatenate([query_ref[:, i * HEAD : (i + 1) * HEAD] for i in range(GROUP)], axis=0)
    scores = lax.dot_general(key_ref[...], queries, (((1,), (1,)), ((), ())), preferred_element_type=jnp.float32)
    weights = []
    for i in range(GROUP):
        mine = scores[:, i * ROWS : (i + 1) * ROWS]
        tiles = [jnp.where(is_causal, mine[:ROWS], mine[ROWS : 2 * ROWS]) + bias_ref[0]]
        tiles += [mine[(t + 1) * ROWS : (t + 2) * ROWS] + bias_ref[t] for t in range(1, 4)]
        peak = jnp.maximum(jnp.maximum(tiles[0], tiles[1]), jnp.maximum(tiles[2], tiles[3]))
        peak = jnp.max(peak, axis=0, keepdims=True)
        raised = [jnp.exp2((tile - peak) * EXP2_SCALE) for tile in tiles]
        near = jnp.where(is_causal, raised[0], 0.0).astype(jnp.bfloat16)
        far = jnp.where(is_causal, 0.0, raised[0]).astype(jnp.bfloat16)
        weights.append(jnp.concatenate([near, far] + [r.astype(jnp.bfloat16) for r in raised[1:]], axis=0))
    blended = jnp.dot(value_ref[...], jnp.concatenate(weights, axis=1), preferred_element_type=jnp.float32)
    result = blended[:HEAD] / blended[HEAD : HEAD + 1]
    for i in range(GROUP):
        at = (out_head + i) * HEAD
        out_ref[:, at : at + HEAD] = result[:, i * ROWS : (i + 1) * ROWS].T.astype(jnp.bfloat16)


def attend_by_query(bias_ref, query_ref, blocks, out_ref, out_head, key_ref, value_ref):
    is_causal = causal()

    @pl.when(pl.program_id(0) == 0)
    def _():
        value_ref[:, HEAD:] = jnp.ones((5 * ROWS, HEAD), jnp.bfloat16)

    for at, (block, key_at, value_at) in enumerate(blocks):
        span = slice(at * ROWS, (at + 1) * ROWS)
        key_ref[span, :] = tile_of(block, key_at)
        value_ref[span, :HEAD] = tile_of(block, value_at)

    def some_heads(step, carry):
        spans = [pl.ds(pl.multiple_of((step * PAIR + i) * HEAD, HEAD), HEAD) for i in range(PAIR)]
        queries = jnp.concatenate([query_ref[:, span] for span in spans], axis=0)
        scores = lax.dot_general(
            queries, key_ref[...], (((1,), (1,)), ((), ())), preferred_element_type=jnp.float32
        )
        weights = []
        for i in range(PAIR):
            mine = scores[i * ROWS : (i + 1) * ROWS]
            tiles = [jnp.where(is_causal, mine[:, :ROWS], mine[:, ROWS : 2 * ROWS]) + bias_ref[0]]
            tiles += [mine[:, (t + 1) * ROWS : (t + 2) * ROWS] + bias_ref[t] for t in range(1, 4)]
            peak = jnp.maximum(jnp.maximum(tiles[0], tiles[1]), jnp.maximum(tiles[2], tiles[3]))
            peak = jnp.max(peak, axis=1, keepdims=True)
            raised = [jnp.exp2((tile - peak) * EXP2_SCALE) for tile in tiles]
            near = jnp.where(is_causal, raised[0], 0.0).astype(jnp.bfloat16)
            far = jnp.where(is_causal, 0.0, raised[0]).astype(jnp.bfloat16)
            weights.append(
                jnp.concatenate([near, far] + [r.astype(jnp.bfloat16) for r in raised[1:]], axis=1)
            )
        blended = jnp.dot(
            jnp.concatenate(weights, axis=0), value_ref[...], preferred_element_type=jnp.float32
        )
        result = (blended[:, :HEAD] / blended[:, HEAD:]).astype(jnp.bfloat16)
        for i in range(PAIR):
            span = pl.ds(pl.multiple_of((out_head + step * PAIR + i) * HEAD, HEAD), HEAD)
            out_ref[:, span] = result[i * ROWS : (i + 1) * ROWS]
        return carry

    lax.fori_loop(0, GROUP // PAIR, some_heads, 0, unroll=2)


ONES = 16
BY_QUERY_SCRATCH = [pltpu.VMEM((5 * ROWS, HEAD), jnp.bfloat16), pltpu.VMEM((5 * ROWS, 2 * HEAD), jnp.bfloat16)]
BY_KEY_SCRATCH = [pltpu.VMEM((5 * ROWS, HEAD), jnp.bfloat16), pltpu.VMEM((HEAD + ONES, 5 * ROWS), jnp.bfloat16)]
OUT = jax.ShapeDtypeStruct((1, 2, ROWS, KV * SPAN), jnp.bfloat16)


def block_specs(first):
    whole = pl.BlockSpec((ROWS, 2 * HEAD), lambda i, *p: (0, first + i))
    return [whole, whole, whole, pl.BlockSpec((2 * ROWS, 2 * HEAD), lambda i, *p: (0, i))]


def near_attention(vmem_limit, by_key, half, stride, count, first, bias, queries, blocks, out_shape, out_spec):
    return pl.pallas_call(
        functools.partial(near_attention_kernel, by_key),
        grid=(count,),
        in_specs=[
            pl.BlockSpec((4, ROWS, ROWS), lambda i: (0, 0, 0)),
            pl.BlockSpec((None, None, ROWS, SPAN), lambda i: (0, half, 0, stride * i)),
        ]
        + block_specs(first),
        out_specs=out_spec,
        scratch_shapes=BY_KEY_SCRATCH if by_key else BY_QUERY_SCRATCH,
        out_shape=out_shape,
        compiler_params=pltpu.CompilerParams(vmem_limit_bytes=vmem_limit),
        cost_estimate=pl.CostEstimate(flops=1 << 20, bytes_accessed=1 << 20, transcendentals=0),
        name="near_attention",
    )(bias, queries, *blocks)


def moved_attention(place, queries, blocks, came, into):
    return pl.pallas_call(
        moved_attention_kernel,
        grid_spec=pltpu.PrefetchScalarGridSpec(
            num_scalar_prefetch=1,
            grid=(MOVED,),
            in_specs=[
                pl.BlockSpec((LABEL_ROWS, HEAD), lambda i, p: (LABELS_AT // LABEL_ROWS, 0)),
                pl.BlockSpec((ROWS, SPAN), lambda i, p: (0, i)),
            ]
            + [pl.BlockSpec((2 * ROWS, HEAD), lambda i, p: (i, 0))] * 5
            + [pl.BlockSpec((ROWS, SPAN), lambda i, p: (0, i)), pl.BlockSpec(memory_space=pl.ANY)],
            out_specs=pl.BlockSpec((None, None, ROWS, 2 * SPAN), lambda i, p: (0, 1, 0, i)),
            scratch_shapes=[pltpu.VMEM((4, ROWS, ROWS), jnp.float32)] + BY_KEY_SCRATCH,
        ),
        out_shape=OUT,
        input_output_aliases={9: 0},
        compiler_params=pltpu.CompilerParams(vmem_limit_bytes=SMALL_VMEM_LIMIT),
        cost_estimate=pl.CostEstimate(flops=1 << 20, bytes_accessed=1 << 20, transcendentals=0),
        name="moved_attention",
    )(place, blocks[0], queries, *blocks, came, into)


def shift(block, step, odd_step=None, wrap=False):
    route = [(s, s + (step if odd_step is None or s % 2 == 0 else odd_step)) for s in range(8)]
    return lax.ppermute(block, "seq", [(s, t % 8) for s, t in route if wrap or t < 8])


def other_core(block):
    return lax.ppermute(block, "seq", [(s, s ^ 1) for s in range(8)])


def exchange(block, far, two, low_core, cols):
    pair = jnp.concatenate([two[:, cols], jnp.where(low_core, block[:, cols], far[:, cols])], axis=0)
    return block, far, two, other_core(pair)


def body(hidden, queries, keys, frozen_values, labels, partner, down, up):
    place = lax.axis_index("seq").astype(jnp.int32)
    low_core = lax.rem(place, 2) == 0
    place = place.reshape((1,))
    mask = jnp.bitwise_xor(partner[0], lax.axis_index("dp"))
    near, kv_moved, moved_queries, bias_zero, bias_one = adapter(
        place, labels, hidden, frozen_values, keys, down.T, up, queries
    )
    near_two, near_far = shift(near, 2, wrap=True), shift(near, 4, wrap=True)

    def route(m):
        return [(r, r ^ m) for r in range(16)]

    def move(m, kv_moved, moved_queries):
        return lax.ppermute(kv_moved, "dp", route(m)), lax.ppermute(moved_queries, "dp", route(m))

    kv_moved, moved_queries = lax.switch(
        mask - 1, [functools.partial(move, m) for m in range(1, 16)], kv_moved, moved_queries
    )
    kv_moved, moved_queries, near_two, near_far = lax.optimization_barrier(
        (kv_moved, moved_queries, near_two, near_far)
    )
    w = shift(kv_moved, 1, 3, wrap=True)
    split = KEPT * 2 * HEAD
    kept_blocks = exchange(near, near_far, near_two, low_core, slice(0, split))
    kept_pair, near_two, near_far = lax.optimization_barrier((kept_blocks[3], near_two, near_far))
    kept_blocks = (near, near_far, near_two, kept_pair)
    zero_blocks = exchange(near, near_far, near_two, low_core, slice(split, None))
    sent = near_attention(
        SMALL_VMEM_LIMIT, True, 1, 2, KEPT, 0, bias_one, queries, kept_blocks,
        jax.ShapeDtypeStruct((ROWS, KEPT * SPAN), jnp.bfloat16), pl.BlockSpec((ROWS, SPAN), lambda i: (0, i)),
    )

    def send(m, sent, kv_moved, bias, queries, *blocks):
        came = lax.ppermute(sent, "dp", route(m))
        two, far, x = shift(kv_moved, 2), shift(kv_moved, 4), shift(kv_moved, 3, 1)
        spec = pl.BlockSpec((None, None, ROWS, SPAN), lambda i: (0, 0, 0, i))
        return came, two, far, x, near_attention(VMEM_LIMIT, False, 0, 1, KV, KEPT, bias, queries, blocks, OUT, spec)

    came, two, far, x, out = lax.switch(
        mask - 1, [functools.partial(send, m) for m in range(1, 16)], sent, kv_moved, bias_zero, queries, *zero_blocks
    )
    moved_blocks = (kv_moved, far, two, x, w)
    return moved_attention(place, moved_queries, moved_blocks, came, out)


def solution(mesh):
    in_specs = (
        P("dp", None, "seq", None),
        P("dp", None, "seq", None),
        P("dp", None, "seq", None),
        P("dp", None, "seq", None),
        P("dp", None, None),
        P("dp"),
        P(),
        P(),
    )
    out_specs = P("dp", None, "seq", None)
    return jax.shard_map(body, mesh=mesh, in_specs=in_specs, out_specs=out_specs, check_vma=False)
```

profile of v0, /device:TPU:1, one launch (start us, length us, event | category | flops | bytes accessed | tf_op | source)
XLA Modules:
  0.0 100.9 jit_solution(15791890606271010002)
XLA Ops:
  0.0 4.5 %adapter.1 = (bf16[128,3072]{1,0:T(8,128)(2,1)S(1)}, bf16[1040,128]{1,0:T(8,128)(2,1)S(1)}, bf16[128,4096]{1,0:T(8,128)(2,1)}, f32[4,128,128]{2,1,0:T(8,128)S(1)}, f32[4,128,128]{2,1,0:T(8,128)}) custom-call(s32[1]{0:T(128)} %bitcast.place_ref, s32[1,2,1024]{2,1,0:T(2,128)} %labels_ref.1, bf16[1,2,128,5120]{3,2,1,0:T(8,128)(2,1)} %hidden_ref.1, ...), custom_call_target="tpu_custom_call" | custom-call | flops 1048576 | bytes 1048576 | tf_op jit(solution)/shard_map/adapter/pallas_call | solution.py:110
  4.5 2.2 %collective-permute-start.90 = (bf16[128,3072]{1,0:T(8,128)(2,1)S(1)}, bf16[128,3072]{1,0:T(8,128)(2,1)S(1)}, u32[]{:S(2)}, u32[]{:S(2)}) collective-permute-start(bf16[128,3072]{1,0:T(8,128)(2,1)S(1)} %get-tuple-element.478.own_ref), channel_id=1, source_target_pairs={{0,2},{1,3},{2,4},{3,5},{4,6},{5,7},{6,0},{7,1},{8,10},{9,11},{10,... | collective-permute-start | bytes 2359304 | tf_op jit(solution)/shard_map/ppermute | solution.py:298
  6.7 2.6 %collective-permute-start.91 = (bf16[128,3072]{1,0:T(8,128)(2,1)S(1)}, bf16[128,3072]{1,0:T(8,128)(2,1)S(1)}, u32[]{:S(2)}, u32[]{:S(2)}) collective-permute-start(bf16[128,3072]{1,0:T(8,128)(2,1)S(1)} %get-tuple-element.478.own_ref), channel_id=1, source_target_pairs={{0,4},{1,5},{2,6},{3,7},{4,0},{5,1},{6,2},{7,3},{8,12},{9,13},{10,... | collective-permute-start | bytes 2359304 | tf_op jit(solution)/shard_map/ppermute | solution.py:298
  10.0 43.3 %conditional.2 = (bf16[1040,128]{1,0:T(8,128)(2,1)}, bf16[128,4096]{1,0:T(8,128)(2,1)}) conditional(s32[]{:T(128)} %clamp.4, (bf16[1040,128]{1,0:T(8,128)(2,1)S(1)}, bf16[128,4096]{1,0:T(8,128)(2,1)}) %tuple.127, (bf16[1040,128]{1,0:T(8,128)(2,1)S(1)}, bf16[128,4096]{1,0:T(8,128)(2,1)}) %tuple.127, ...), branch_computations={%region_0.0_spmd, %region_1.0_spmd, %region_2.0_spmd, %region_3.0_... | conditional | bytes 5259360 | solution.py:326
  10.0 8.6 %collective-permute-start.29 = (bf16[128,4096]{1,0:T(8,128)(2,1)}, bf16[128,4096]{1,0:T(8,128)(2,1)}, u32[]{:S(2)}, u32[]{:S(2)}) collective-permute-start(bf16[128,4096]{1,0:T(8,128)(2,1)} %get-tuple-element.334), channel_id=1, source_target_pairs={{0,120},{8,112},{16,104},{24,96},{32,88},{40,80},{48,72},{56,64},{... | collective-permute-start | bytes 3145736 | tf_op jit(solution)/shard_map/cond/branch_14_fun/ppermute | solution.py:324
  18.6 5.4 %collective-permute-start.28 = (bf16[1040,128]{1,0:T(8,128)(2,1)S(1)}, bf16[1040,128]{1,0:T(8,128)(2,1)}, u32[]{:S(2)}, u32[]{:S(2)}) collective-permute-start(bf16[1040,128]{1,0:T(8,128)(2,1)S(1)} %get-tuple-element.333), channel_id=1, source_target_pairs={{0,120},{8,112},{16,104},{24,96},{32,88},{40,80},{48,72},{56,64},{... | collective-permute-start | bytes 798728 | tf_op jit(solution)/shard_map/cond/branch_14_fun/ppermute | solution.py:324
  24.1 29.3 %collective-permute-done.28 = bf16[1040,128]{1,0:T(8,128)(2,1)} collective-permute-done((bf16[1040,128]{1,0:T(8,128)(2,1)S(1)}, bf16[1040,128]{1,0:T(8,128)(2,1)}, u32[]{:S(2)}, u32[]{:S(2)}) %collective-permute-start.28) | collective-permute-done | bytes 266272 | tf_op jit(solution)/shard_map/cond/branch_14_fun/ppermute | solution.py:324
  53.3 0.0 collective-permute-done.29
  53.3 0.0 collective-permute-done.90.two_ref
  53.3 0.0 collective-permute-done.91.far_ref
  53.3 0.0 copy-start.1
  53.4 1.0 collective-permute-start.92
  54.4 1.5 %collective-permute-done.92.pair_ref = bf16[256,1024]{1,0:T(8,128)(2,1)S(1)} collective-permute-done((bf16[256,1024]{1,0:T(8,128)(2,1)S(1)}, bf16[256,1024]{1,0:T(8,128)(2,1)S(1)}, u32[]{:S(2)}, u32[]{:S(2)}) %collective-permute-start.92) | collective-permute-done | bytes 524320 | tf_op jit(solution)/shard_map/ppermute | solution.py:302
  55.9 0.1 slice_select_fusion
  56.0 0.1 pad_maximum_fusion
  56.2 0.5 collective-permute-start.93
  56.6 3.0 %collective-permute-start.94 = (bf16[1040,128]{1,0:T(8,128)(2,1)}, bf16[1040,128]{1,0:T(8,128)(2,1)S(1)}, u32[]{:S(2)}, u32[]{:S(2)}) collective-permute-start(bf16[1040,128]{1,0:T(8,128)(2,1)} %get-tuple-element.479.label_ref.own_ref), channel_id=1, source_target_pairs={{0,1},{1,4},{2,3},{3,6},{4,5},{5,0},{6,7},{7,2},{8,9},{9,12},{10,1... | collective-permute-start | bytes 798728 | tf_op jit(solution)/shard_map/ppermute | solution.py:298
  59.6 0.0 copy-done
  59.6 7.2 %near_attention.31 = bf16[128,4096]{1,0:T(8,128)(2,1)} custom-call(f32[4,128,128]{2,1,0:T(8,128)S(1)} %copy-done, bf16[1,2,128,8192]{3,2,1,0:T(8,128)(2,1)} %query_ref.1, bf16[128,3072]{1,0:T(8,128)(2,1)S(1)} %get-tuple-element.478.own_ref, bf16[128,3072]{1,0:T(8,128)(2,1)} %copy-done.1, bf16[128,3072]{1,0:T(8,128)(2,1)S(1)} %collective-permute-done.90.two_ref, ...), custom_call_target="tpu_custom_call" | custom-call | flops 1048576 | bytes 1048576 | tf_op jit(solution)/shard_map/near_attention/pallas_call | solution.py:256
  66.8 0.0 collective-permute-done.93
  66.8 26.5 %conditional.3 = (bf16[128,4096]{1,0:T(8,128)(2,1)}, bf16[1040,128]{1,0:T(8,128)(2,1)}, bf16[1040,128]{1,0:T(8,128)(2,1)}, bf16[1040,128]{1,0:T(8,128)(2,1)}, bf16[1,2,128,8192]{3,2,1,0:T(8,128)(2,1)}) conditional(s32[]{:T(128)} %clamp.4, (bf16[128,4096]{1,0:T(8,128)(2,1)}, bf16[1040,128]{1,0:T(8,128)(2,1)}, ...), branch_computations={%region_15.16_spmd, %region_16.17_spmd, %region_17.18_spmd, %regio... | conditional | flops 1048576 | bytes 8437960 | solution.py:349
  66.8 0.0 collective-permute-start.86
  66.8 3.0 %collective-permute-start.87 = (bf16[1040,128]{1,0:T(8,128)(2,1)}, bf16[1040,128]{1,0:T(8,128)(2,1)}, u32[]{:S(2)}, u32[]{:S(2)}) collective-permute-start(bf16[1040,128]{1,0:T(8,128)(2,1)} %get-tuple-element.448), channel_id=1, source_target_pairs={{0,2},{1,3},{2,4},{3,5},{4,6},{5,7},{8,10},{9,11},{10,12},{11,13},... | collective-permute-start | bytes 798728 | tf_op jit(solution)/shard_map/cond/branch_14_fun/ppermute | solution.py:298
  69.8 3.6 %collective-permute-start.88 = (bf16[1040,128]{1,0:T(8,128)(2,1)}, bf16[1040,128]{1,0:T(8,128)(2,1)}, u32[]{:S(2)}, u32[]{:S(2)}) collective-permute-start(bf16[1040,128]{1,0:T(8,128)(2,1)} %get-tuple-element.448), channel_id=1, source_target_pairs={{0,4},{1,5},{2,6},{3,7},{8,12},{9,13},{10,14},{11,15},{16,20},{17,... | collective-permute-start | bytes 798728 | tf_op jit(solution)/shard_map/cond/branch_14_fun/ppermute | solution.py:298
  73.3 2.0 %collective-permute-start.89 = (bf16[1040,128]{1,0:T(8,128)(2,1)}, bf16[1040,128]{1,0:T(8,128)(2,1)}, u32[]{:S(2)}, u32[]{:S(2)}) collective-permute-start(bf16[1040,128]{1,0:T(8,128)(2,1)} %get-tuple-element.448), channel_id=1, source_target_pairs={{0,3},{1,2},{2,5},{3,4},{4,7},{5,6},{8,11},{9,10},{10,13},{11,12},... | collective-permute-start | bytes 798728 | tf_op jit(solution)/shard_map/cond/branch_14_fun/ppermute | solution.py:298
  75.3 15.7 %near_attention.30 = bf16[1,2,128,8192]{3,2,1,0:T(8,128)(2,1)} custom-call(f32[4,128,128]{2,1,0:T(8,128)S(1)} %get-tuple-element.449.bias_ref, bf16[1,2,128,8192]{3,2,1,0:T(8,128)(2,1)} %get-tuple-element.450.query_ref, bf16[128,3072]{1,0:T(8,128)(2,1)S(1)} %get-tuple-element.451.own_ref, bf16[128,3072]{1,0:T(8,128)(2,1)} %get-tuple-element.452.far_ref, ...), custom_call_target="tpu_custom_call" | custom-call | flops 1048576 | bytes 1048576 | tf_op jit(solution)/shard_map/cond/branch_14_fun/near_attention/pallas_call | solution.py:256
  91.0 0.0 collective-permute-done.87
  91.0 0.0 collective-permute-done.88
  91.0 0.0 collective-permute-done.89
  91.0 2.3 %collective-permute-done.86 = bf16[128,4096]{1,0:T(8,128)(2,1)} collective-permute-done((bf16[128,4096]{1,0:T(8,128)(2,1)}, bf16[128,4096]{1,0:T(8,128)(2,1)}, u32[]{:S(2)}, u32[]{:S(2)}) %collective-permute-start.86) | collective-permute-done | bytes 1048608 | tf_op jit(solution)/shard_map/cond/branch_14_fun/ppermute | solution.py:344
  93.3 0.0 collective-permute-done.94.w_ref
  93.3 7.6 %moved_attention.1 = bf16[1,2,128,8192]{3,2,1,0:T(8,128)(2,1)} custom-call(s32[1]{0:T(128)} %bitcast.place_ref, bf16[1040,128]{1,0:T(8,128)(2,1)} %get-tuple-element.479.label_ref.own_ref, bf16[128,4096]{1,0:T(8,128)(2,1)} %get-tuple-element.480.query_ref, bf16[1040,128]{1,0:T(8,128)(2,1)} %get-tuple-element.479.label_ref.own_ref, ...), custom_call_target="tpu_custom_call", output_to_operand_aliasing={{}: (9, {})} | custom-call | flops 1048576 | bytes 1048576 | tf_op jit(solution)/shard_map/moved_attention/pallas_call | solution.py:274
  (6 shorter events, 0.1 us)
Async XLA Ops:
  4.5 55.1 %copy-start = (f32[4,128,128]{2,1,0:T(8,128)S(1)}, f32[4,128,128]{2,1,0:T(8,128)}, u32[]{:S(2)}) copy-start(f32[4,128,128]{2,1,0:T(8,128)} %get-tuple-element.481.bias_ref) | copy-start | bytes 786436
  4.5 48.8 %collective-permute-start.90 = (bf16[128,3072]{1,0:T(8,128)(2,1)S(1)}, bf16[128,3072]{1,0:T(8,128)(2,1)S(1)}, u32[]{:S(2)}, u32[]{:S(2)}) collective-permute-start(bf16[128,3072]{1,0:T(8,128)(2,1)S(1)} %get-tuple-element.478.own_ref), channel_id=1, source_target_pairs={{0,2},{1,3},{2,4},{3,5},{4,6},{5,7},{6,0},{7,1},{8,10},{9,11},{10,... | collective-permute-start | bytes 2359304 | tf_op jit(solution)/shard_map/ppermute | solution.py:298
  6.7 46.6 %collective-permute-start.91 = (bf16[128,3072]{1,0:T(8,128)(2,1)S(1)}, bf16[128,3072]{1,0:T(8,128)(2,1)S(1)}, u32[]{:S(2)}, u32[]{:S(2)}) collective-permute-start(bf16[128,3072]{1,0:T(8,128)(2,1)S(1)} %get-tuple-element.478.own_ref), channel_id=1, source_target_pairs={{0,4},{1,5},{2,6},{3,7},{4,0},{5,1},{6,2},{7,3},{8,12},{9,13},{10,... | collective-permute-start | bytes 2359304 | tf_op jit(solution)/shard_map/ppermute | solution.py:298
  10.0 43.3 %collective-permute-start.29 = (bf16[128,4096]{1,0:T(8,128)(2,1)}, bf16[128,4096]{1,0:T(8,128)(2,1)}, u32[]{:S(2)}, u32[]{:S(2)}) collective-permute-start(bf16[128,4096]{1,0:T(8,128)(2,1)} %get-tuple-element.334), channel_id=1, source_target_pairs={{0,120},{8,112},{16,104},{24,96},{32,88},{40,80},{48,72},{56,64},{... | collective-permute-start | bytes 3145736 | tf_op jit(solution)/shard_map/cond/branch_14_fun/ppermute | solution.py:324
  18.6 34.7 %collective-permute-start.28 = (bf16[1040,128]{1,0:T(8,128)(2,1)S(1)}, bf16[1040,128]{1,0:T(8,128)(2,1)}, u32[]{:S(2)}, u32[]{:S(2)}) collective-permute-start(bf16[1040,128]{1,0:T(8,128)(2,1)S(1)} %get-tuple-element.333), channel_id=1, source_target_pairs={{0,120},{8,112},{16,104},{24,96},{32,88},{40,80},{48,72},{56,64},{... | collective-permute-start | bytes 798728 | tf_op jit(solution)/shard_map/cond/branch_14_fun/ppermute | solution.py:324
  53.3 2.7 %copy-start.1 = (bf16[128,3072]{1,0:T(8,128)(2,1)}, bf16[128,3072]{1,0:T(8,128)(2,1)S(1)}, u32[]{:S(2)}) copy-start(bf16[128,3072]{1,0:T(8,128)(2,1)S(1)} %collective-permute-done.91.far_ref) | copy-start | bytes 2359300
  53.4 2.5 %collective-permute-start.92 = (bf16[256,1024]{1,0:T(8,128)(2,1)S(1)}, bf16[256,1024]{1,0:T(8,128)(2,1)S(1)}, u32[]{:S(2)}, u32[]{:S(2)}) collective-permute-start(bf16[256,1024]{1,0:T(8,128)(2,1)S(1)} %pad_maximum_fusion.1), channel_id=1, source_target_pairs={{0,1},{1,0},{2,3},{3,2},{4,5},{5,4},{6,7},{7,6},{8,9},{9,8},{10,11... | collective-permute-start | bytes 1572872 | tf_op jit(solution)/shard_map/ppermute | solution.py:302
  56.2 10.6 %collective-permute-start.93 = (bf16[256,2048]{1,0:T(8,128)(2,1)S(1)}, bf16[256,2048]{1,0:T(8,128)(2,1)S(1)}, u32[]{:S(2)}, u32[]{:S(2)}) collective-permute-start(bf16[256,2048]{1,0:T(8,128)(2,1)S(1)} %pad_maximum_fusion), channel_id=1, source_target_pairs={{0,1},{1,0},{2,3},{3,2},{4,5},{5,4},{6,7},{7,6},{8,9},{9,8},{10,11... | collective-permute-start | bytes 3145736 | tf_op jit(solution)/shard_map/ppermute | solution.py:302
  56.6 36.7 %collective-permute-start.94 = (bf16[1040,128]{1,0:T(8,128)(2,1)}, bf16[1040,128]{1,0:T(8,128)(2,1)S(1)}, u32[]{:S(2)}, u32[]{:S(2)}) collective-permute-start(bf16[1040,128]{1,0:T(8,128)(2,1)} %get-tuple-element.479.label_ref.own_ref), channel_id=1, source_target_pairs={{0,1},{1,4},{2,3},{3,6},{4,5},{5,0},{6,7},{7,2},{8,9},{9,12},{10,1... | collective-permute-start | bytes 798728 | tf_op jit(solution)/shard_map/ppermute | solution.py:298
  66.8 26.5 %collective-permute-start.86 = (bf16[128,4096]{1,0:T(8,128)(2,1)}, bf16[128,4096]{1,0:T(8,128)(2,1)}, u32[]{:S(2)}, u32[]{:S(2)}) collective-permute-start(bf16[128,4096]{1,0:T(8,128)(2,1)} %get-tuple-element.447), channel_id=1, source_target_pairs={{0,120},{8,112},{16,104},{24,96},{32,88},{40,80},{48,72},{56,64},{... | collective-permute-start | bytes 3145736 | tf_op jit(solution)/shard_map/cond/branch_14_fun/ppermute | solution.py:344
  66.8 24.2 %collective-permute-start.87 = (bf16[1040,128]{1,0:T(8,128)(2,1)}, bf16[1040,128]{1,0:T(8,128)(2,1)}, u32[]{:S(2)}, u32[]{:S(2)}) collective-permute-start(bf16[1040,128]{1,0:T(8,128)(2,1)} %get-tuple-element.448), channel_id=1, source_target_pairs={{0,2},{1,3},{2,4},{3,5},{4,6},{5,7},{8,10},{9,11},{10,12},{11,13},... | collective-permute-start | bytes 798728 | tf_op jit(solution)/shard_map/cond/branch_14_fun/ppermute | solution.py:298
  69.8 21.2 %collective-permute-start.88 = (bf16[1040,128]{1,0:T(8,128)(2,1)}, bf16[1040,128]{1,0:T(8,128)(2,1)}, u32[]{:S(2)}, u32[]{:S(2)}) collective-permute-start(bf16[1040,128]{1,0:T(8,128)(2,1)} %get-tuple-element.448), channel_id=1, source_target_pairs={{0,4},{1,5},{2,6},{3,7},{8,12},{9,13},{10,14},{11,15},{16,20},{17,... | collective-permute-start | bytes 798728 | tf_op jit(solution)/shard_map/cond/branch_14_fun/ppermute | solution.py:298
  73.3 17.7 %collective-permute-start.89 = (bf16[1040,128]{1,0:T(8,128)(2,1)}, bf16[1040,128]{1,0:T(8,128)(2,1)}, u32[]{:S(2)}, u32[]{:S(2)}) collective-permute-start(bf16[1040,128]{1,0:T(8,128)(2,1)} %get-tuple-element.448), channel_id=1, source_target_pairs={{0,3},{1,2},{2,5},{3,4},{4,7},{5,6},{8,11},{9,10},{10,13},{11,12},... | collective-permute-start | bytes 798728 | tf_op jit(solution)/shard_map/cond/branch_14_fun/ppermute | solution.py:298
where the time goes:
time: 99.1 us; the launch traced here: 101 us
  Pallas kernels  35 us (35%)
  waiting for transfers between devices  33.1 us (33%)
  starting transfers between devices  31.7 us (32%)
    ppermute x1, waiting for transfers between devices, move(): lax.ppermute(kv_moved, 'dp', route(m))  29.3 us
    pallas_call x2, Pallas kernels, near_attention(): pl.pallas_call(functools.partial(near_attention_kernel, by_key), grid=(co...  22.9 us
    ppermute x6, starting transfers between devices, shift(): lax.ppermute(block, 'seq', [(s, t % 8) for s, t in route if wrap or t < 8])  16.3 us
    ppermute x1, starting transfers between devices, move(): lax.ppermute(moved_queries, 'dp', route(m))  8.59 us
    pallas_call x1, Pallas kernels, moved_attention(): pl.pallas_call(moved_attention_kernel, grid_spec=pltpu.PrefetchScalarGrid...  7.64 us
    ppermute x1, starting transfers between devices, move(): lax.ppermute(kv_moved, 'dp', route(m))  5.42 us
    pallas_call x1, Pallas kernels, adapter(): pl.pallas_call(adapter_kernel, grid_spec=pltpu.PrefetchScalarGridSpec(num...  4.51 us
    ppermute x1, waiting for transfers between devices, send(): came = lax.ppermute(sent, 'dp', route(m))  2.28 us
  transfers between devices with their start and end apart: 11, of which 3 were waited for; matrix products, arithmetic and copies ran while one was open for 0% of the time, Pallas kernels for 23%

commit v1 on v0

--- a/solution.py
+++ b/solution.py
@@ -244,7 +244,7 @@
 ONES = 16
 BY_QUERY_SCRATCH = [pltpu.VMEM((5 * ROWS, HEAD), jnp.bfloat16), pltpu.VMEM((5 * ROWS, 2 * HEAD), jnp.bfloat16)]
 BY_KEY_SCRATCH = [pltpu.VMEM((5 * ROWS, HEAD), jnp.bfloat16), pltpu.VMEM((HEAD + ONES, 5 * ROWS), jnp.bfloat16)]
-OUT = jax.ShapeDtypeStruct((1, 2, ROWS, KV * SPAN), jnp.bfloat16)
+OUT = pltpu.HBM((1, 2, ROWS, KV * SPAN), jnp.bfloat16)
 
 
 def block_specs(first):
@@ -293,9 +293,13 @@
     )(place, blocks[0], queries, *blocks, came, into)
 
 
-def shift(block, step, odd_step=None, wrap=False):
+def shift(block, step, odd_step=None):
     route = [(s, s + (step if odd_step is None or s % 2 == 0 else odd_step)) for s in range(8)]
-    return lax.ppermute(block, "seq", [(s, t % 8) for s, t in route if wrap or t < 8])
+    return lax.ppermute(block, "seq", [(s, t) for s, t in route if t < 8])
+
+
+def full_shift(block, targets):
+    return lax.ppermute(block, "seq", list(enumerate(targets)))
 
 
 def other_core(block):
@@ -315,7 +319,7 @@
     near, kv_moved, moved_queries, bias_zero, bias_one = adapter(
         place, labels, hidden, frozen_values, keys, down.T, up, queries
     )
-    near_two, near_far = shift(near, 2, wrap=True), shift(near, 4, wrap=True)
+    near_two, near_far = full_shift(near, (2, 3, 4, 5, 6, 7, 0, 1)), full_shift(near, (4, 5, 6, 7, 2, 3, 0, 1))
 
     def route(m):
         return [(r, r ^ m) for r in range(16)]
@@ -329,7 +333,7 @@
     kv_moved, moved_queries, near_two, near_far = lax.optimization_barrier(
         (kv_moved, moved_queries, near_two, near_far)
     )
-    w = shift(kv_moved, 1, 3, wrap=True)
+    x = full_shift(kv_moved, (3, 2, 5, 4, 7, 6, 1, 0))
     split = KEPT * 2 * HEAD
     kept_blocks = exchange(near, near_far, near_two, low_core, slice(0, split))
     kept_pair, near_two, near_far = lax.optimization_barrier((kept_blocks[3], near_two, near_far))
@@ -342,11 +346,11 @@
 
     def send(m, sent, kv_moved, bias, queries, *blocks):
         came = lax.ppermute(sent, "dp", route(m))
-        two, far, x = shift(kv_moved, 2), shift(kv_moved, 4), shift(kv_moved, 3, 1)
+        two, far, w = shift(kv_moved, 2), shift(kv_moved, 4), shift(kv_moved, 1, 3)
         spec = pl.BlockSpec((None, None, ROWS, SPAN), lambda i: (0, 0, 0, i))
-        return came, two, far, x, near_attention(VMEM_LIMIT, False, 0, 1, KV, KEPT, bias, queries, blocks, OUT, spec)
-
-    came, two, far, x, out = lax.switch(
+        return came, two, far, w, near_attention(44 << 20, False, 0, 1, KV, KEPT, bias, queries, blocks, OUT, spec)
+
+    came, two, far, w, out = lax.switch(
         mask - 1, [functools.partial(send, m) for m in range(1, 16)], sent, kv_moved, bias_zero, queries, *zero_blocks
     )
     moved_blocks = (kv_moved, far, two, x, w)

time: 99.1 us -> 87.7 us (0.88); the launches traced: 101 us -> 87.7 us
  starting transfers between devices: 31.7 us -> 20.7 us
  waiting for transfers between devices: 33.1 us -> 31.8 us
  Pallas kernels: 35 us -> 33.8 us
    ppermute x1, starting transfers between devices: 8.59 us -> 1.72 us  [move(): lax.ppermute(moved_queries, 'dp', route(m))]
    ppermute x1, starting transfers between devices: 5.42 us -> 0.09 us  [move(): lax.ppermute(kv_moved, 'dp', route(m))]
    ppermute x1, waiting for transfers between devices: 2.28 us -> 0.01 us  [send(): came = lax.ppermute(sent, 'dp', route(m))]
    ppermute x6, waiting for transfers between devices: 0.02 us -> 2.23 us  [the longest x3 2.23 us: full_shift(): return lax.ppermute(block, 'seq', list(enumerate(targets)))]
    ppermute x1, starting transfers between devices: 0.01 us -> 1.72 us  [send(): came = lax.ppermute(sent, 'dp', route(m))]
    pallas_call x2, Pallas kernels: 22.9 us -> 21.7 us  [near_attention(): pl.pallas_call(functools.partial(near_attention_kernel, by_key), grid=(co...]
    ppermute x1, waiting for transfers between devices: 29.3 us -> 28.1 us  [move(): lax.ppermute(kv_moved, 'dp', route(m))]
    ppermute x6, starting transfers between devices: 16.3 us -> 15.2 us  [the longest x3 10.4 us: shift(): return lax.ppermute(block, 'seq', [(s, t) for s, t in route if t < 8])]
  transfers between devices with their start and end apart: 11 -> 11, of which waited for: 3 -> 3; matrix products, arithmetic and copies ran while one was open for 0% -> 0% of each run, Pallas kernels for 23% -> 25%
where the time goes in v1:
time: 87.7 us
  Pallas kernels  33.8 us (39%)
  waiting for transfers between devices  31.8 us (36%)
  starting transfers between devices  20.7 us (24%)
    ppermute x1, waiting for transfers between devices, move(): lax.ppermute(kv_moved, 'dp', route(m))  28.1 us
    pallas_call x2, Pallas kernels, near_attention(): pl.pallas_call(functools.partial(near_attention_kernel, by_key), grid=(co...  21.7 us
    ppermute x3, starting transfers between devices, shift(): return lax.ppermute(block, 'seq', [(s, t) for s, t in route if t < 8])  10.4 us
    pallas_call x1, Pallas kernels, moved_attention(): pl.pallas_call(moved_attention_kernel, grid_spec=pltpu.PrefetchScalarGrid...  7.63 us
    ppermute x3, starting transfers between devices, full_shift(): return lax.ppermute(block, 'seq', list(enumerate(targets)))  4.82 us
    pallas_call x1, Pallas kernels, adapter(): pl.pallas_call(adapter_kernel, grid_spec=pltpu.PrefetchScalarGridSpec(num...  4.5 us
    ppermute x3, waiting for transfers between devices, full_shift(): return lax.ppermute(block, 'seq', list(enumerate(targets)))  2.23 us
    ppermute x2, starting transfers between devices, other_core(): return lax.ppermute(block, 'seq', [(s, s ^ 1) for s in range(8)])  1.9 us
  transfers between devices with their start and end apart: 11, of which 3 were waited for; matrix products, arithmetic and copies ran while one was open for 0% of the time, Pallas kernels for 25%

profile of v1, /device:TPU:1, one launch (start us, length us, event | category | flops | bytes accessed | tf_op | source)
XLA Modules:
  0.0 87.7 jit_solution(15138384103163400257)
XLA Ops:
  0.0 4.5 %adapter.1 = (bf16[128,3072]{1,0:T(8,128)(2,1)S(1)}, bf16[1040,128]{1,0:T(8,128)(2,1)S(1)}, bf16[128,4096]{1,0:T(8,128)(2,1)}, f32[4,128,128]{2,1,0:T(8,128)S(1)}, f32[4,128,128]{2,1,0:T(8,128)}) custom-call(s32[1]{0:T(128)} %bitcast.place_ref, s32[1,2,1024]{2,1,0:T(2,128)} %labels_ref.1, bf16[1,2,128,5120]{3,2,1,0:T(8,128)(2,1)} %hidden_ref.1, ...), custom_call_target="tpu_custom_call" | custom-call | flops 1048576 | bytes 1048576 | tf_op jit(solution)/shard_map/adapter/pallas_call | solution.py:110
  4.5 2.2 %collective-permute-start.90 = (bf16[128,3072]{1,0:T(8,128)(2,1)S(1)}, bf16[128,3072]{1,0:T(8,128)(2,1)S(1)}, u32[]{:S(2)}, u32[]{:S(2)}) collective-permute-start(bf16[128,3072]{1,0:T(8,128)(2,1)S(1)} %get-tuple-element.478.own_ref), channel_id=1, source_target_pairs={{0,2},{1,3},{2,4},{3,5},{4,6},{5,7},{6,0},{7,1},{8,10},{9,11},{10,... | collective-permute-start | bytes 2359304 | tf_op jit(solution)/shard_map/ppermute | solution.py:302
  6.7 2.6 %collective-permute-start.91 = (bf16[128,3072]{1,0:T(8,128)(2,1)S(1)}, bf16[128,3072]{1,0:T(8,128)(2,1)S(1)}, u32[]{:S(2)}, u32[]{:S(2)}) collective-permute-start(bf16[128,3072]{1,0:T(8,128)(2,1)S(1)} %get-tuple-element.478.own_ref), channel_id=1, source_target_pairs={{0,4},{1,5},{2,6},{3,7},{4,2},{5,3},{6,0},{7,1},{8,12},{9,13},{10,... | collective-permute-start | bytes 2359304 | tf_op jit(solution)/shard_map/ppermute | solution.py:302
  10.0 29.9 %conditional.2 = (bf16[1040,128]{1,0:T(8,128)(2,1)}, bf16[128,4096]{1,0:T(8,128)(2,1)}) conditional(s32[]{:T(128)} %clamp.4, (bf16[1040,128]{1,0:T(8,128)(2,1)S(1)}, bf16[128,4096]{1,0:T(8,128)(2,1)}) %tuple.127, (bf16[1040,128]{1,0:T(8,128)(2,1)S(1)}, bf16[128,4096]{1,0:T(8,128)(2,1)}) %tuple.127, ...), branch_computations={%region_0.0_spmd, %region_1.0_spmd, %region_2.0_spmd, %region_3.0_... | conditional | bytes 5259360 | solution.py:330
  10.0 1.7 %collective-permute-start.7 = (bf16[128,4096]{1,0:T(8,128)(2,1)}, bf16[128,4096]{1,0:T(8,128)(2,1)}, u32[]{:S(2)}, u32[]{:S(2)}) collective-permute-start(bf16[128,4096]{1,0:T(8,128)(2,1)} %get-tuple-element.312), channel_id=1, source_target_pairs={{0,32},{8,40},{16,48},{24,56},{32,0},{40,8},{48,16},{56,24},{64,96... | collective-permute-start | bytes 3145736 | tf_op jit(solution)/shard_map/cond/branch_3_fun/ppermute | solution.py:328
  11.7 0.1 collective-permute-start.6
  11.8 28.1 %collective-permute-done.6 = bf16[1040,128]{1,0:T(8,128)(2,1)} collective-permute-done((bf16[1040,128]{1,0:T(8,128)(2,1)S(1)}, bf16[1040,128]{1,0:T(8,128)(2,1)}, u32[]{:S(2)}, u32[]{:S(2)}) %collective-permute-start.6) | collective-permute-done | bytes 266272 | tf_op jit(solution)/shard_map/cond/branch_3_fun/ppermute | solution.py:328
  39.9 0.0 collective-permute-done.7
  39.9 0.0 collective-permute-done.90.two_ref
  39.9 2.2 %collective-permute-done.91.far_ref = bf16[128,3072]{1,0:T(8,128)(2,1)S(1)} collective-permute-done((bf16[128,3072]{1,0:T(8,128)(2,1)S(1)}, bf16[128,3072]{1,0:T(8,128)(2,1)S(1)}, u32[]{:S(2)}, u32[]{:S(2)}) %collective-permute-start.91) | collective-permute-done | bytes 786464 | tf_op jit(solution)/shard_map/ppermute | solution.py:302
  42.2 1.4 %collective-permute-start.92 = (bf16[256,1024]{1,0:T(8,128)(2,1)S(1)}, bf16[256,1024]{1,0:T(8,128)(2,1)S(1)}, u32[]{:S(2)}, u32[]{:S(2)}) collective-permute-start(bf16[256,1024]{1,0:T(8,128)(2,1)S(1)} %pad_maximum_fusion.1), channel_id=1, source_target_pairs={{0,1},{1,0},{2,3},{3,2},{4,5},{5,4},{6,7},{7,6},{8,9},{9,8},{10,11... | collective-permute-start | bytes 1572872 | tf_op jit(solution)/shard_map/ppermute | solution.py:306
  43.7 1.5 %collective-permute-done.92.pair_ref = bf16[256,1024]{1,0:T(8,128)(2,1)S(1)} collective-permute-done((bf16[256,1024]{1,0:T(8,128)(2,1)S(1)}, bf16[256,1024]{1,0:T(8,128)(2,1)S(1)}, u32[]{:S(2)}, u32[]{:S(2)}) %collective-permute-start.92) | collective-permute-done | bytes 524320 | tf_op jit(solution)/shard_map/ppermute | solution.py:306
  45.2 0.1 slice_select_fusion
  45.3 0.0 copy-done.2
  45.3 0.1 pad_maximum_fusion
  45.4 0.5 collective-permute-start.93
  45.9 0.0 collective-permute-start.94
  45.9 0.0 copy-start.3
  45.9 6.5 %near_attention.31 = bf16[128,4096]{1,0:T(8,128)(2,1)S(1)} custom-call(f32[4,128,128]{2,1,0:T(8,128)S(1)} %copy-done, bf16[1,2,128,8192]{3,2,1,0:T(8,128)(2,1)S(1)} %copy-done.1, bf16[128,3072]{1,0:T(8,128)(2,1)S(1)} %get-tuple-element.478.own_ref, bf16[128,3072]{1,0:T(8,128)(2,1)} %copy-done.2, bf16[128,3072]{1,0:T(8,128)(2,1)S(1)} %collective-permute-done.90.two_ref, ...), custom_call_target="tpu_custom_call" | custom-call | flops 1048576 | bytes 1048576 | tf_op jit(solution)/shard_map/near_attention/pallas_call | solution.py:256
  52.5 0.0 collective-permute-done.93
  52.5 27.6 %conditional.3 = (bf16[128,4096]{1,0:T(8,128)(2,1)}, bf16[1040,128]{1,0:T(8,128)(2,1)}, bf16[1040,128]{1,0:T(8,128)(2,1)}, bf16[1040,128]{1,0:T(8,128)(2,1)}, bf16[1,2,128,8192]{3,2,1,0:T(8,128)(2,1)}) conditional(s32[]{:T(128)} %clamp.4, (bf16[128,4096]{1,0:T(8,128)(2,1)S(1)}, bf16[1040,128]{1,0:T(8,128)(2,1)}, ...), branch_computations={%region_15.16_spmd, %region_16.17_spmd, %region_17.18_spmd, %regio... | conditional | flops 1048576 | bytes 8437960 | solution.py:353
  52.5 1.7 %collective-permute-start.42 = (bf16[128,4096]{1,0:T(8,128)(2,1)S(1)}, bf16[128,4096]{1,0:T(8,128)(2,1)}, u32[]{:S(2)}, u32[]{:S(2)}) collective-permute-start(bf16[128,4096]{1,0:T(8,128)(2,1)S(1)} %get-tuple-element.359), channel_id=1, source_target_pairs={{0,32},{8,40},{16,48},{24,56},{32,0},{40,8},{48,16},{56,24},{64,96... | collective-permute-start | bytes 3145736 | tf_op jit(solution)/shard_map/cond/branch_3_fun/ppermute | solution.py:348
  54.3 4.0 %collective-permute-start.43 = (bf16[1040,128]{1,0:T(8,128)(2,1)}, bf16[1040,128]{1,0:T(8,128)(2,1)}, u32[]{:S(2)}, u32[]{:S(2)}) collective-permute-start(bf16[1040,128]{1,0:T(8,128)(2,1)} %get-tuple-element.360), channel_id=1, source_target_pairs={{0,2},{1,3},{2,4},{3,5},{4,6},{5,7},{8,10},{9,11},{10,12},{11,13},... | collective-permute-start | bytes 798728 | tf_op jit(solution)/shard_map/cond/branch_3_fun/ppermute | solution.py:298
  58.3 4.5 %collective-permute-start.44 = (bf16[1040,128]{1,0:T(8,128)(2,1)}, bf16[1040,128]{1,0:T(8,128)(2,1)}, u32[]{:S(2)}, u32[]{:S(2)}) collective-permute-start(bf16[1040,128]{1,0:T(8,128)(2,1)} %get-tuple-element.360), channel_id=1, source_target_pairs={{0,4},{1,5},{2,6},{3,7},{8,12},{9,13},{10,14},{11,15},{16,20},{17,... | collective-permute-start | bytes 798728 | tf_op jit(solution)/shard_map/cond/branch_3_fun/ppermute | solution.py:298
  62.8 1.9 %collective-permute-start.45 = (bf16[1040,128]{1,0:T(8,128)(2,1)}, bf16[1040,128]{1,0:T(8,128)(2,1)}, u32[]{:S(2)}, u32[]{:S(2)}) collective-permute-start(bf16[1040,128]{1,0:T(8,128)(2,1)} %get-tuple-element.360), channel_id=1, source_target_pairs={{0,1},{1,4},{2,3},{3,6},{4,5},{6,7},{8,9},{9,12},{10,11},{11,14},{... | collective-permute-start | bytes 798728 | tf_op jit(solution)/shard_map/cond/branch_3_fun/ppermute | solution.py:298
  64.7 15.1 %near_attention.19 = bf16[1,2,128,8192]{3,2,1,0:T(8,128)(2,1)} custom-call(f32[4,128,128]{2,1,0:T(8,128)S(1)} %get-tuple-element.361.bias_ref, bf16[1,2,128,8192]{3,2,1,0:T(8,128)(2,1)S(1)} %get-tuple-element.362.query_ref, bf16[128,3072]{1,0:T(8,128)(2,1)S(1)} %get-tuple-element.363.own_ref, bf16[128,3072]{1,0:T(8,128)(2,1)S(1)} %get-tuple-element.364.far_ref, ...), custom_call_target="tpu_custom_call" | custom-call | flops 1048576 | bytes 1048576 | tf_op jit(solution)/shard_map/cond/branch_3_fun/near_attention/pallas_call | solution.py:256
  79.8 0.0 collective-permute-done.43
  79.8 0.0 collective-permute-done.44
  79.8 0.0 collective-permute-done.45
  79.8 0.0 collective-permute-done.42
  80.1 0.0 collective-permute-done.94.x_ref
  80.1 7.6 %moved_attention.1 = bf16[1,2,128,8192]{3,2,1,0:T(8,128)(2,1)} custom-call(s32[1]{0:T(128)} %bitcast.place_ref, bf16[1040,128]{1,0:T(8,128)(2,1)} %get-tuple-element.479.label_ref.own_ref, bf16[128,4096]{1,0:T(8,128)(2,1)} %get-tuple-element.480.query_ref, bf16[1040,128]{1,0:T(8,128)(2,1)} %get-tuple-element.479.label_ref.own_ref, ...), custom_call_target="tpu_custom_call", output_to_operand_aliasing={{}: (9, {})} | custom-call | flops 1048576 | bytes 1048576 | tf_op jit(solution)/shard_map/moved_attention/pallas_call | solution.py:274
  (10 shorter events, 0.1 us)
Async XLA Ops:
  4.5 41.4 %copy-start = (f32[4,128,128]{2,1,0:T(8,128)S(1)}, f32[4,128,128]{2,1,0:T(8,128)}, u32[]{:S(2)}) copy-start(f32[4,128,128]{2,1,0:T(8,128)} %get-tuple-element.481.bias_ref) | copy-start | bytes 786436
  4.5 35.4 %collective-permute-start.90 = (bf16[128,3072]{1,0:T(8,128)(2,1)S(1)}, bf16[128,3072]{1,0:T(8,128)(2,1)S(1)}, u32[]{:S(2)}, u32[]{:S(2)}) collective-permute-start(bf16[128,3072]{1,0:T(8,128)(2,1)S(1)} %get-tuple-element.478.own_ref), channel_id=1, source_target_pairs={{0,2},{1,3},{2,4},{3,5},{4,6},{5,7},{6,0},{7,1},{8,10},{9,11},{10,... | collective-permute-start | bytes 2359304 | tf_op jit(solution)/shard_map/ppermute | solution.py:302
  6.7 35.4 %collective-permute-start.91 = (bf16[128,3072]{1,0:T(8,128)(2,1)S(1)}, bf16[128,3072]{1,0:T(8,128)(2,1)S(1)}, u32[]{:S(2)}, u32[]{:S(2)}) collective-permute-start(bf16[128,3072]{1,0:T(8,128)(2,1)S(1)} %get-tuple-element.478.own_ref), channel_id=1, source_target_pairs={{0,4},{1,5},{2,6},{3,7},{4,2},{5,3},{6,0},{7,1},{8,12},{9,13},{10,... | collective-permute-start | bytes 2359304 | tf_op jit(solution)/shard_map/ppermute | solution.py:302
  10.0 29.9 %collective-permute-start.7 = (bf16[128,4096]{1,0:T(8,128)(2,1)}, bf16[128,4096]{1,0:T(8,128)(2,1)}, u32[]{:S(2)}, u32[]{:S(2)}) collective-permute-start(bf16[128,4096]{1,0:T(8,128)(2,1)} %get-tuple-element.312), channel_id=1, source_target_pairs={{0,32},{8,40},{16,48},{24,56},{32,0},{40,8},{48,16},{56,24},{64,96... | collective-permute-start | bytes 3145736 | tf_op jit(solution)/shard_map/cond/branch_3_fun/ppermute | solution.py:328
  11.7 28.2 %collective-permute-start.6 = (bf16[1040,128]{1,0:T(8,128)(2,1)S(1)}, bf16[1040,128]{1,0:T(8,128)(2,1)}, u32[]{:S(2)}, u32[]{:S(2)}) collective-permute-start(bf16[1040,128]{1,0:T(8,128)(2,1)S(1)} %get-tuple-element.311), channel_id=1, source_target_pairs={{0,32},{8,40},{16,48},{24,56},{32,0},{40,8},{48,16},{56,24},{64,96... | collective-permute-start | bytes 798728 | tf_op jit(solution)/shard_map/cond/branch_3_fun/ppermute | solution.py:328
  39.9 6.0 %copy-start.1 = (bf16[1,2,128,8192]{3,2,1,0:T(8,128)(2,1)S(1)}, bf16[1,2,128,8192]{3,2,1,0:T(8,128)(2,1)}, u32[]{:S(2)}) copy-start(bf16[1,2,128,8192]{3,2,1,0:T(8,128)(2,1)} %query_ref.1) | copy-start | bytes 12582916
  42.1 3.2 %copy-start.2 = (bf16[128,3072]{1,0:T(8,128)(2,1)}, bf16[128,3072]{1,0:T(8,128)(2,1)S(1)}, u32[]{:S(2)}) copy-start(bf16[128,3072]{1,0:T(8,128)(2,1)S(1)} %collective-permute-done.91.far_ref) | copy-start | bytes 2359300
  42.2 3.0 %collective-permute-start.92 = (bf16[256,1024]{1,0:T(8,128)(2,1)S(1)}, bf16[256,1024]{1,0:T(8,128)(2,1)S(1)}, u32[]{:S(2)}, u32[]{:S(2)}) collective-permute-start(bf16[256,1024]{1,0:T(8,128)(2,1)S(1)} %pad_maximum_fusion.1), channel_id=1, source_target_pairs={{0,1},{1,0},{2,3},{3,2},{4,5},{5,4},{6,7},{7,6},{8,9},{9,8},{10,11... | collective-permute-start | bytes 1572872 | tf_op jit(solution)/shard_map/ppermute | solution.py:306
  45.4 7.0 %collective-permute-start.93 = (bf16[256,2048]{1,0:T(8,128)(2,1)S(1)}, bf16[256,2048]{1,0:T(8,128)(2,1)S(1)}, u32[]{:S(2)}, u32[]{:S(2)}) collective-permute-start(bf16[256,2048]{1,0:T(8,128)(2,1)S(1)} %pad_maximum_fusion), channel_id=1, source_target_pairs={{0,1},{1,0},{2,3},{3,2},{4,5},{5,4},{6,7},{7,6},{8,9},{9,8},{10,11... | collective-permute-start | bytes 3145736 | tf_op jit(solution)/shard_map/ppermute | solution.py:306
  45.9 34.2 %collective-permute-start.94 = (bf16[1040,128]{1,0:T(8,128)(2,1)}, bf16[1040,128]{1,0:T(8,128)(2,1)S(1)}, u32[]{:S(2)}, u32[]{:S(2)}) collective-permute-start(bf16[1040,128]{1,0:T(8,128)(2,1)} %get-tuple-element.479.label_ref.own_ref), channel_id=1, source_target_pairs={{0,3},{1,2},{2,5},{3,4},{4,7},{5,6},{6,1},{7,0},{8,11},{9,10},{10,... | collective-permute-start | bytes 798728 | tf_op jit(solution)/shard_map/ppermute | solution.py:302
  45.9 6.6 %copy-start.3 = (bf16[128,3072]{1,0:T(8,128)(2,1)S(1)}, bf16[128,3072]{1,0:T(8,128)(2,1)}, u32[]{:S(2)}) copy-start(bf16[128,3072]{1,0:T(8,128)(2,1)} %copy-done.2) | copy-start | bytes 2359300
  52.5 27.3 %collective-permute-start.42 = (bf16[128,4096]{1,0:T(8,128)(2,1)S(1)}, bf16[128,4096]{1,0:T(8,128)(2,1)}, u32[]{:S(2)}, u32[]{:S(2)}) collective-permute-start(bf16[128,4096]{1,0:T(8,128)(2,1)S(1)} %get-tuple-element.359), channel_id=1, source_target_pairs={{0,32},{8,40},{16,48},{24,56},{32,0},{40,8},{48,16},{56,24},{64,96... | collective-permute-start | bytes 3145736 | tf_op jit(solution)/shard_map/cond/branch_3_fun/ppermute | solution.py:348
  54.3 25.5 %collective-permute-start.43 = (bf16[1040,128]{1,0:T(8,128)(2,1)}, bf16[1040,128]{1,0:T(8,128)(2,1)}, u32[]{:S(2)}, u32[]{:S(2)}) collective-permute-start(bf16[1040,128]{1,0:T(8,128)(2,1)} %get-tuple-element.360), channel_id=1, source_target_pairs={{0,2},{1,3},{2,4},{3,5},{4,6},{5,7},{8,10},{9,11},{10,12},{11,13},... | collective-permute-start | bytes 798728 | tf_op jit(solution)/shard_map/cond/branch_3_fun/ppermute | solution.py:298
  58.3 21.5 %collective-permute-start.44 = (bf16[1040,128]{1,0:T(8,128)(2,1)}, bf16[1040,128]{1,0:T(8,128)(2,1)}, u32[]{:S(2)}, u32[]{:S(2)}) collective-permute-start(bf16[1040,128]{1,0:T(8,128)(2,1)} %get-tuple-element.360), channel_id=1, source_target_pairs={{0,4},{1,5},{2,6},{3,7},{8,12},{9,13},{10,14},{11,15},{16,20},{17,... | collective-permute-start | bytes 798728 | tf_op jit(solution)/shard_map/cond/branch_3_fun/ppermute | solution.py:298
  62.8 17.0 %collective-permute-start.45 = (bf16[1040,128]{1,0:T(8,128)(2,1)}, bf16[1040,128]{1,0:T(8,128)(2,1)}, u32[]{:S(2)}, u32[]{:S(2)}) collective-permute-start(bf16[1040,128]{1,0:T(8,128)(2,1)} %get-tuple-element.360), channel_id=1, source_target_pairs={{0,1},{1,4},{2,3},{3,6},{4,5},{6,7},{8,9},{9,12},{10,11},{11,14},{... | collective-permute-start | bytes 798728 | tf_op jit(solution)/shard_map/cond/branch_3_fun/ppermute | solution.py:298
